TPU v7x, 256 devices: a whole 4x4x8 slice. The times are simulated.
256 devices in a mesh: row: 16 (over y, x), col: 8 (over z), vox: 2 (over core).
Axes of the slice: x: 4, y: 4, z: 8, core: 2. Of those that a mesh axis runs over, the one named last changes fastest.
Arguments:
- coeffs_r: bfloat16 [32, 16, 64, 2, 1024], P(None, 'row', None, None, 'col'), may hold values from -0.125 to 0.125
- rhs: bfloat16 [32, 16, 64, 1536], P('col', 'row', None, 'vox'), may hold values from -6 to 6
- inverses: bfloat16 [2, 1024, 1024], replicated, may hold values from -0.1875 to 0.1875
Outputs:
- updated: bfloat16 [32, 16, 64, 1536], P('col', 'row', None, 'vox')
All inputs are finite; a program needn't handle non-finite values.
Results may differ from a plain program's by a relative error of at most 0.0049.
Values may be sent and summed in bfloat16 or wider, within the bound.
A program may use at most 64 MiB of HBM per device.

v0:
```python
import jax
import jax.numpy as jnp
from jax import lax
from jax.sharding import PartitionSpec as P


def spread(value, axis, root):
    mine = lax.axis_index(axis) == root
    return lax.psum(jnp.where(mine, value, jnp.zeros_like(value)), axis)


def solve_block(inverse, rhs_block, col_pos, own_cols):
    solved_all = jnp.dot(inverse, rhs_block, preferred_element_type=jnp.float32).astype(
        jnp.bfloat16
    )
    solved_mine = lax.dynamic_slice_in_dim(solved_all, col_pos * own_cols, own_cols, 0)
    return (solved_all, solved_mine)


def local(coeffs_r, rhs, inverses):
    row_count = lax.axis_size("row")
    col_count = lax.axis_size("col")
    row_pos = lax.axis_index("row")
    col_pos = lax.axis_index("col")
    per_col = rhs.shape[0]
    block_rows = rhs.shape[2]
    voxels = rhs.shape[3]
    cycles = coeffs_r.shape[0]
    own_cols = coeffs_r.shape[4]
    block_order = inverses.shape[1]
    tail_cycles = block_order // (block_rows * row_count)
    owner_col = col_count - 1
    tail_piece = rhs[per_col - tail_cycles :]
    tail_rows = lax.all_gather(tail_piece, "row", axis=1, tiled=True)
    tail_rows = spread(tail_rows, "col", owner_col)
    solved_last, last_mine = solve_block(
        inverses[1], tail_rows.reshape(block_order, voxels), col_pos, own_cols
    )
    panel_rows = coeffs_r[cycles - 2 * tail_cycles : cycles - tail_cycles, 0, :, 1, :]
    panel_rows = panel_rows.reshape(tail_cycles * block_rows, own_cols)
    partial_value = -jnp.dot(panel_rows, last_mine, preferred_element_type=jnp.float32)
    known = rhs[per_col - 2 * tail_cycles : per_col - tail_cycles, 0]
    known = known.reshape(tail_cycles * block_rows, voxels).astype(jnp.float32)
    partial_value = partial_value + jnp.where(col_pos == owner_col, known, jnp.zeros_like(known))
    partial_value = partial_value.reshape(tail_cycles, 1, block_rows, voxels)
    padded = jnp.zeros((tail_cycles, row_count, block_rows, voxels), jnp.float32)
    anchor = jnp.zeros((), jnp.int32)
    padded = lax.dynamic_update_slice(padded, partial_value, (anchor, row_pos, anchor, anchor))
    middle_rhs = lax.psum(padded, ("row", "col")).astype(jnp.bfloat16)
    solved_first, first_mine = solve_block(
        inverses[0], middle_rhs.reshape(block_order, voxels), col_pos, own_cols
    )
    stacked_mine = jnp.stack([first_mine, last_mine])
    removed = lax.psum_scatter(
        jnp.einsum("kprjc,jcv->kprv", coeffs_r, stacked_mine, preferred_element_type=jnp.float32),
        "col",
        scatter_dimension=0,
        tiled=True,
    )
    remaining = (rhs.astype(jnp.float32) - removed).astype(jnp.bfloat16)

    def my_rows(solved):
        shaped = solved.reshape(tail_cycles, row_count, block_rows, voxels)
        return lax.dynamic_slice_in_dim(shaped, row_pos, 1, 1)

    window = jnp.concatenate([my_rows(solved_first), my_rows(solved_last)], 0)
    lower_part = jnp.where(col_pos == owner_col, window, remaining[per_col - 2 * tail_cycles :])
    return jnp.concatenate([remaining[: per_col - 2 * tail_cycles], lower_part], 0)


def solution(mesh):
    placed = (P(None, "row", None, None, "col"), P("col", "row", None, "vox"), P())
    return jax.shard_map(
        local, mesh=mesh, in_specs=placed, out_specs=P("col", "row", None, "vox"), check_vma=False
    )
```

profile of v0, /device:TPU:1, one launch (start us, length us, event | category | flops | bytes accessed | tf_op | source)
XLA Modules:
  0.0 951.8 jit_solution(15609546226498273052)
XLA Ops:
  6.5 0.0 all-gather.2.cloned.1.call-start
  6.5 1.5 slice.28
  8.1 0.0 all-gather.2.cloned.1.call-update
  8.1 0.0 all-reduce.3.cloned.1.call-start
  8.2 53.5 %all-gather.2.cloned.1.call-done = bf16[1,16,64,768]{3,2,0,1:T(8,128)(2,1)} async-done(((bf16[1,1,64,768]{3,2,0,1:T(8,128)(2,1)}), bf16[1,16,64,768]{3,2,0,1:T(8,128)(2,1)}) %all-gather.2.cloned.1.call-update) | async-done | bytes 1572880 | tf_op jit(solution)/shard_map/all_gather | solution.py:34
  61.6 1.3 broadcast_select_fusion
  62.9 0.0 all-reduce.3.cloned.1.call-update
  62.9 0.0 reduce-scatter.2.cloned.1.call-start
  63.0 1.4 slice.23
  64.4 75.1 %all-reduce.3.cloned.1.call-done = bf16[1024,768]{1,0:T(8,128)(2,1)} async-done(((bf16[1024,768]{1,0:T(8,128)(2,1)}), bf16[1024,768]{1,0:T(8,128)(2,1)}) %all-reduce.3.cloned.1.call-update) | async-done | bytes 1572880 | tf_op jit(solution)/shard_map/psum | solution.py:9
  139.5 3.9 fusion.6
  143.4 0.0 copy-start
  143.4 0.8 dynamic-slice_bitcast_fusion.1
  144.3 0.3 broadcast_in_dim.9
  144.6 0.0 copy-done
  144.6 0.6 copy-done.3
  145.2 0.0 copy-done.5
  145.2 0.2 fusion.15
  145.5 610.3 %all-reduce.4 = bf16[1,16,64,768]{3,2,1,0:T(8,128)(2,1)} all-reduce(f32[1,16,64,768]{3,2,1,0:T(8,128)S(1)} %fusion.15), channel_id=1, replica_groups=mesh['row'=16,'col'=8,'vox'=2] {'row','col'}, use_global_device_ids=true, to_apply=%region_1.2 | all-reduce | flops 786432 | bytes 4718592 | tf_op jit(solution)/shard_map/psum | solution.py:49
  755.8 4.0 fusion.9
  759.8 0.1 dynamic-slice_bitcast_fusion
  759.9 0.0 copy-done.2
  759.9 0.0 copy-done.4
  759.9 3.7 convolution_bitcast_fusion
  763.6 0.0 reduce-scatter.2.cloned.1.call-update
  763.6 1.4 copy-done.1
  765.0 1.6 copy.26
  766.5 0.7 copy.24
  767.2 0.9 constant_dynamic-slice_fusion
  768.1 175.1 %reduce-scatter.2.cloned.1.call-done = f32[4,1,64,768]{3,2,0,1:T(8,128)} async-done(((f32[32,1,64,768]{3,2,0,1:T(8,128)}), f32[4,1,64,768]{3,2,0,1:T(8,128)}) %reduce-scatter.2.cloned.1.call-update) | async-done | bytes 786448 | tf_op jit(solution)/shard_map/reduce_scatter | solution.py:54
  943.3 1.2 subtract_convert_fusion
  944.5 0.8 maximum_bitcast_fusion.2
  (7 shorter events, 0.1 us)
Async XLA Ops:
  6.5 55.1 %all-gather.2.cloned.1.call-start = ((), (), s32[]{:S(2)}) async-start(), calls=%async_computation.1 | async-start | bytes 1671168 | tf_op jit(solution)/shard_map/all_gather | solution.py:34
  8.1 131.4 %all-reduce.3.cloned.1.call-start = ((), (), s32[]{:S(2)}) async-start(), calls=%async_computation.2 | async-start | bytes 3145728 | tf_op jit(solution)/shard_map/psum | solution.py:9
  62.9 880.4 %reduce-scatter.2.cloned.1.call-start = ((), (), s32[]{:S(2)}) async-start(), calls=%async_computation.3 | async-start | bytes 7077888 | tf_op jit(solution)/shard_map/reduce_scatter | solution.py:54
  143.4 1.2 copy-start
  144.3 1.0 copy-start.3
  144.3 1.0 copy-start.5
  755.8 4.1 copy-start.2
  755.8 4.1 copy-start.4
  763.6 1.4 copy-start.1
Sparse Core Ops, SparseCore 0:
  9.8 51.8 all-gather.1
  64.0 75.4 all-reduce.2
  763.7 179.5 reduce-scatter.1
where the time goes:
time: 952 us
  blocking collectives  610 us (64%)
  waiting for transfers between devices  304 us (32%)
  between operations  13.2 us (1%)
  matrix products  11.8 us (1%)
    psum x1, blocking collectives, local(): middle_rhs = lax.psum(padded, ('row', 'col')).astype(jnp.bfloat16)  610 us
    reduce_scatter x1, waiting for transfers between devices, local(): lax.psum_scatter(jnp.einsum('kprjc,jcv->kprv', coeffs_r, stacked_mine, pr...  175 us
    psum x1, waiting for transfers between devices, spread(): return lax.psum(jnp.where(mine, value, jnp.zeros_like(value)), axis)  75.1 us
    all_gather x1, waiting for transfers between devices, local(): tail_rows = lax.all_gather(tail_piece, 'row', axis=1, tiled=True)  53.5 us
  transfers between devices with their start and end apart: 3, of which 3 were waited for; matrix products, arithmetic and copies ran while one was open for 0% of the time, Pallas kernels for 0%

commit v1 on v0

--- a/solution.py
+++ b/solution.py
@@ -2,6 +2,10 @@
 import jax.numpy as jnp
 from jax import lax
 from jax.sharding import PartitionSpec as P
+
+
+def draw_spots(inp):
+    return lax.psum(lax.psum(inp, axis_name="col"), "row")
 
 
 def spread(value, axis, root):
@@ -46,7 +50,7 @@
     padded = jnp.zeros((tail_cycles, row_count, block_rows, voxels), jnp.float32)
     anchor = jnp.zeros((), jnp.int32)
     padded = lax.dynamic_update_slice(padded, partial_value, (anchor, row_pos, anchor, anchor))
-    middle_rhs = lax.psum(padded, ("row", "col")).astype(jnp.bfloat16)
+    middle_rhs = draw_spots(padded).astype(jnp.bfloat16)
     solved_first, first_mine = solve_block(
         inverses[0], middle_rhs.reshape(block_order, voxels), col_pos, own_cols
     )

time: 952 us -> 424 us (0.45)
  blocking collectives: 610 us -> 86.1 us
    psum x1, blocking collectives: 610 us -> 86.1 us  [draw_spots(): return lax.psum(lax.psum(inp, axis_name='col'), 'row')]
    reduce_scatter x1, waiting for transfers between devices: 175 us -> 75.5 us  [local(): lax.psum_scatter(jnp.einsum('kprjc,jcv->kprv', coeffs_r, stacked_mine, pr...]
    psum x0 -> x1, waiting for transfers between devices: none -> 92.4 us  [draw_spots(): return lax.psum(lax.psum(inp, axis_name='col'), 'row')]
  transfers between devices with their start and end apart: 3 -> 4, of which waited for: 3 -> 4; matrix products, arithmetic and copies ran while one was open for 0% -> 2% of each run, Pallas kernels for 0% -> 0%
where the time goes in v1:
time: 424 us; the launch traced here: 423 us
  waiting for transfers between devices  297 us (70%)
  blocking collectives  86.1 us (20%)
  between operations  13.3 us (3%)
  local copies, waits for them, and re-layouts  12.8 us (3%)
  matrix products  11.3 us (3%)
    psum x1, waiting for transfers between devices, draw_spots(): return lax.psum(lax.psum(inp, axis_name='col'), 'row')  92.4 us
    psum x1, blocking collectives, draw_spots(): return lax.psum(lax.psum(inp, axis_name='col'), 'row')  86.1 us
    reduce_scatter x1, waiting for transfers between devices, local(): lax.psum_scatter(jnp.einsum('kprjc,jcv->kprv', coeffs_r, stacked_mine, pr...  75.5 us
    psum x1, waiting for transfers between devices, spread(): return lax.psum(jnp.where(mine, value, jnp.zeros_like(value)), axis)  75.1 us
    all_gather x1, waiting for transfers between devices, local(): tail_rows = lax.all_gather(tail_piece, 'row', axis=1, tiled=True)  53.5 us
  transfers between devices with their start and end apart: 4, of which 4 were waited for; matrix products, arithmetic and copies ran while one was open for 2% of the time, Pallas kernels for 0%

profile of v1, /device:TPU:1, one launch (start us, length us, event | category | flops | bytes accessed | tf_op | source)
XLA Modules:
  0.0 423.4 jit_solution(16092534142462679838)
XLA Ops:
  6.5 1.5 slice.28
  8.1 0.0 all-gather.2.cloned.1.call-update
  8.1 0.0 all-reduce.4.cloned.1.call-start
  8.2 53.5 %all-gather.2.cloned.1.call-done = bf16[1,16,64,768]{3,2,0,1:T(8,128)(2,1)} async-done(((bf16[1,1,64,768]{3,2,0,1:T(8,128)(2,1)}), bf16[1,16,64,768]{3,2,0,1:T(8,128)(2,1)}) %all-gather.2.cloned.1.call-update) | async-done | bytes 1572880 | tf_op jit(solution)/shard_map/all_gather | solution.py:38
  61.6 1.3 broadcast_select_fusion
  62.9 0.0 all-reduce.4.cloned.1.call-update
  62.9 0.0 all-reduce.6.cloned.1.call-start
  63.0 1.4 slice.23
  64.4 75.1 %all-reduce.4.cloned.1.call-done = bf16[1024,768]{1,0:T(8,128)(2,1)} async-done(((bf16[1024,768]{1,0:T(8,128)(2,1)}), bf16[1024,768]{1,0:T(8,128)(2,1)}) %all-reduce.4.cloned.1.call-update) | async-done | bytes 1572880 | tf_op jit(solution)/shard_map/psum | solution.py:13
  139.5 3.9 fusion.6
  143.4 0.0 copy-start.4
  143.4 0.3 broadcast_in_dim.9
  143.7 0.8 copy-done.1
  144.6 0.1 copy-done.4
  144.7 0.2 fusion.15
  144.9 1.7 copy-done
  146.6 0.0 all-reduce.6.cloned.1.call-update
  146.6 0.0 reduce-scatter.2.cloned.1.call-start
  146.7 1.6 dynamic-slice_bitcast_fusion.1
  148.3 92.4 %all-reduce.6.cloned.1.call-done = f32[1,16,64,768]{3,2,1,0:T(8,128)} async-done(((f32[1,16,64,768]{3,2,1,0:T(8,128)}), f32[1,16,64,768]{3,2,1,0:T(8,128)}) %all-reduce.6.cloned.1.call-update) | async-done | bytes 3145744 | tf_op jit(solution)/shard_map/psum | solution.py:8
  240.7 86.1 %all-reduce.7 = bf16[1,16,64,768]{3,2,1,0:T(8,128)(2,1)S(1)} all-reduce(f32[1,16,64,768]{3,2,1,0:T(8,128)} %all-reduce.6.cloned.1.call-done), channel_id=1, replica_groups=mesh['row'=16,'col'=8,'vox'=2] {'row'}, use_global_device_ids=true, to_apply=%region_2.3 | all-reduce | flops 786432 | bytes 4718592 | tf_op jit(solution)/shard_map/psum | solution.py:8
  326.8 3.5 fusion.9
  330.3 0.1 dynamic-slice_bitcast_fusion
  330.4 3.7 convolution_bitcast_fusion
  334.1 0.0 reduce-scatter.2.cloned.1.call-update
  334.1 1.4 copy-done.2
  335.5 1.6 copy.26
  337.1 1.5 constant_dynamic-slice_fusion
  338.6 0.7 copy.24
  339.4 75.5 %reduce-scatter.2.cloned.1.call-done = f32[4,1,64,768]{3,2,0,1:T(8,128)} async-done(((f32[32,1,64,768]{3,2,0,1:T(8,128)}), f32[4,1,64,768]{3,2,0,1:T(8,128)}) %reduce-scatter.2.cloned.1.call-update) | async-done | bytes 786448 | tf_op jit(solution)/shard_map/reduce_scatter | solution.py:58
  414.9 1.2 subtract_convert_fusion
  416.1 0.8 maximum_bitcast_fusion.2
  (14 shorter events, 0.1 us)
Async XLA Ops:
  6.5 55.1 %all-gather.2.cloned.1.call-start = ((), (), s32[]{:S(2)}) async-start(), calls=%async_computation.1 | async-start | bytes 1671168 | tf_op jit(solution)/shard_map/all_gather | solution.py:38
  8.1 131.4 %all-reduce.4.cloned.1.call-start = ((), (), s32[]{:S(2)}) async-start(), calls=%async_computation.2 | async-start | bytes 3145728 | tf_op jit(solution)/shard_map/psum | solution.py:13
  62.9 177.8 %all-reduce.6.cloned.1.call-start = ((), (), s32[]{:S(2)}) async-start(), calls=%async_computation.3 | async-start | bytes 6291456 | tf_op jit(solution)/shard_map/psum | solution.py:8
  143.4 1.2 copy-start.1
  143.4 1.3 copy-start.4
  143.4 1.3 copy-start.7
  144.9 1.7 copy-start
  146.6 268.2 %reduce-scatter.2.cloned.1.call-start = ((), (), s32[]{:S(2)}) async-start(), calls=%async_computation.4 | async-start | bytes 7077888 | tf_op jit(solution)/shard_map/reduce_scatter | solution.py:58
  326.8 3.6 copy-start.3
  326.8 3.6 copy-start.5
  334.1 1.4 copy-start.2
  339.3 76.7 %copy-start.6 = (bf16[1,1,64,768]{3,2,0,1:T(8,128)(2,1)S(1)}, bf16[1,1,64,768]{3,2,0,1:T(8,128)(2,1)}, u32[]{:S(2)}) copy-start(bf16[1,1,64,768]{3,2,0,1:T(8,128)(2,1)} %constant_dynamic-slice_fusion) | copy-start | bytes 294916
Sparse Core Ops, SparseCore 0:
  9.8 51.8 all-gather.1
  64.0 75.4 all-reduce.3
  146.7 93.8 all-reduce.5
  334.3 80.5 reduce-scatter.1

commit v2 on v0

--- a/solution.py
+++ b/solution.py
@@ -31,7 +31,15 @@
     tail_cycles = block_order // (block_rows * row_count)
     owner_col = col_count - 1
     tail_piece = rhs[per_col - tail_cycles :]
-    tail_rows = lax.all_gather(tail_piece, "row", axis=1, tiled=True)
+
+    def zone_follow(w_in):
+        met_up = lax.all_to_all(
+            jnp.stack([w_in for _ in range(lax.psum(1, axis_name="row"))]), "row", 0, 0
+        )
+        low = jnp.concatenate(met_up, axis=1)
+        return low
+
+    tail_rows = zone_follow(tail_piece)
     tail_rows = spread(tail_rows, "col", owner_col)
     solved_last, last_mine = solve_block(
         inverses[1], tail_rows.reshape(block_order, voxels), col_pos, own_cols

time: 952 us -> 929 us (0.976)
  waiting for transfers between devices: 304 us -> 272 us
    all_gather x1 -> x0, waiting for transfers between devices: 53.5 us -> none  [local(): tail_rows = lax.all_gather(tail_piece, 'row', axis=1, tiled=True)]
    all_to_all x0 -> x1, waiting for transfers between devices: none -> 22.8 us  [zone_follow(): lax.all_to_all(jnp.stack([w_in for _ in range(lax.psum(1, axis_name='row'...]
where the time goes in v2:
time: 929 us
  blocking collectives  610 us (66%)
  waiting for transfers between devices  272 us (29%)
  between operations  13.5 us (1%)
  matrix products  11.8 us (1%)
  local copies, waits for them, and re-layouts  10 us (1%)
    psum x1, blocking collectives, local(): middle_rhs = lax.psum(padded, ('row', 'col')).astype(jnp.bfloat16)  610 us
    reduce_scatter x1, waiting for transfers between devices, local(): lax.psum_scatter(jnp.einsum('kprjc,jcv->kprv', coeffs_r, stacked_mine, pr...  175 us
    psum x1, waiting for transfers between devices, spread(): return lax.psum(jnp.where(mine, value, jnp.zeros_like(value)), axis)  74.4 us
    all_to_all x1, waiting for transfers between devices, zone_follow(): lax.all_to_all(jnp.stack([w_in for _ in range(lax.psum(1, axis_name='row'...  22.8 us
  transfers between devices with their start and end apart: 3, of which 3 were waited for; matrix products, arithmetic and copies ran while one was open for 0% of the time, Pallas kernels for 0%

profile of v2, /device:TPU:1, one launch (start us, length us, event | category | flops | bytes accessed | tf_op | source)
XLA Modules:
  0.0 929.0 jit_solution(2832155144976847634)
XLA Ops:
  6.5 0.9 slice_bitcast_fusion
  7.4 1.3 stack.8
  8.7 7.6 all-to-all-start
  16.3 0.0 all-reduce.3.cloned.1.call-start
  16.4 22.8 %all-to-all-done = bf16[16,1,1,64,768]{4,3,2,1,0:T(8,128)(2,1)S(1)} async-done(((bf16[16,1,1,64,768]{4,3,2,1,0:T(8,128)(2,1)}), bf16[16,1,1,64,768]{4,3,2,1,0:T(8,128)(2,1)S(1)}, u32[]{:S(2)}, u32[]{:S(2)}) %all-to-all-start) | async-done | bytes 1572896 | tf_op jit(solution)/shard_map/all_to_all | solution.py:36
  39.2 1.3 broadcast_select_fusion
  40.5 0.0 all-reduce.3.cloned.1.call-update
  40.5 0.0 reduce-scatter.2.cloned.1.call-start
  40.6 1.4 slice.26
  42.0 74.4 %all-reduce.3.cloned.1.call-done = bf16[1024,768]{1,0:T(8,128)(2,1)} async-done(((bf16[1024,768]{1,0:T(8,128)(2,1)}), bf16[1024,768]{1,0:T(8,128)(2,1)}) %all-reduce.3.cloned.1.call-update) | async-done | bytes 1572880 | tf_op jit(solution)/shard_map/psum | solution.py:9
  116.4 3.9 fusion.6
  120.3 0.0 copy-start
  120.3 0.8 dynamic-slice_bitcast_fusion.1
  121.1 0.3 broadcast_in_dim.9
  121.4 0.1 copy-done
  121.5 0.6 copy-done.3
  122.1 0.0 copy-done.5
  122.1 0.2 fusion.15
  122.3 610.3 %all-reduce.4 = bf16[1,16,64,768]{3,2,1,0:T(8,128)(2,1)} all-reduce(f32[1,16,64,768]{3,2,1,0:T(8,128)S(1)} %fusion.15), channel_id=1, replica_groups=mesh['row'=16,'col'=8,'vox'=2] {'row','col'}, use_global_device_ids=true, to_apply=%region_1.2 | all-reduce | flops 786432 | bytes 4718592 | tf_op jit(solution)/shard_map/psum | solution.py:57
  732.6 4.0 fusion.9
  736.6 0.1 dynamic-slice_bitcast_fusion
  736.7 0.0 copy-done.2
  736.7 0.0 copy-done.4
  736.7 3.7 convolution_bitcast_fusion
  740.4 0.0 reduce-scatter.2.cloned.1.call-update
  740.4 1.4 copy-done.1
  741.8 1.6 copy.16
  743.4 0.7 copy.14
  744.1 0.9 constant_dynamic-slice_fusion
  745.0 175.2 %reduce-scatter.2.cloned.1.call-done = f32[4,1,64,768]{3,2,0,1:T(8,128)} async-done(((f32[32,1,64,768]{3,2,0,1:T(8,128)}), f32[4,1,64,768]{3,2,0,1:T(8,128)}) %reduce-scatter.2.cloned.1.call-update) | async-done | bytes 786448 | tf_op jit(solution)/shard_map/reduce_scatter | solution.py:62
  920.1 1.2 subtract_convert_fusion
  921.4 0.8 maximum_bitcast_fusion.2
  (7 shorter events, 0.1 us)
Async XLA Ops:
  8.7 30.5 %all-to-all-start = ((bf16[16,1,1,64,768]{4,3,2,1,0:T(8,128)(2,1)}), bf16[16,1,1,64,768]{4,3,2,1,0:T(8,128)(2,1)S(1)}, u32[]{:S(2)}, u32[]{:S(2)}) async-start(bf16[16,1,1,64,768]{4,3,2,1,0:T(8,128)(2,1)} %stack.8), calls=%async_computation | async-start | bytes 3145728 | tf_op jit(solution)/shard_map/all_to_all | solution.py:36
  16.3 100.0 %all-reduce.3.cloned.1.call-start = ((), (), s32[]{:S(2)}) async-start(), calls=%async_computation.2 | async-start | bytes 3145728 | tf_op jit(solution)/shard_map/psum | solution.py:9
  40.5 879.6 %reduce-scatter.2.cloned.1.call-start = ((), (), s32[]{:S(2)}) async-start(), calls=%async_computation.3 | async-start | bytes 7077888 | tf_op jit(solution)/shard_map/reduce_scatter | solution.py:62
  120.3 1.2 copy-start
  121.1 1.0 copy-start.3
  121.1 1.0 copy-start.5
  732.6 4.1 copy-start.2
  732.6 4.1 copy-start.4
  740.4 1.4 copy-start.1
Sparse Core Ops, SparseCore 0:
  40.6 75.6 all-reduce.2
  740.6 179.5 reduce-scatter.1
